TPU v7x, 768 devices: a whole 4x8x12 slice. The times are simulated.
768 devices in a mesh: row: 192 (over y, z, core), col: 4 (over x).
Axes of the slice: x: 4, y: 8, z: 12, core: 2. Of those that a mesh axis runs over, the one named last changes fastest.
Arguments:
- amplitudes: bfloat16 [96, 576, 2500], P(None, 'row'), may hold values from -6 to 6
- integrals: bfloat16 [3072, 200, 2500], P(('row', 'col')), may hold values from -0.125 to 0.125
- cd_tile: int32 [4], replicated, may hold values from 0 to 95
- target: int32 [3072], replicated, may hold values from 0 to 3
- counts: int32 [768], replicated, may hold values from 1 to 4, as said below
Outputs:
- residual: float32 [768, 576, 200], P(('row', 'col'))
Inputs may be any that keep to these rules, and one draw needn't show every extreme that they name: `counts`: some device has 4 live slots.
All inputs are finite; a program needn't handle non-finite values.
Results may differ from a plain program's by a relative error of at most 0.0003.
Values may be sent and summed in bfloat16 or wider, within the bound.
A program may use at most 64 MiB of HBM per device.

v0:
```python
import jax
import jax.numpy as jnp
from jax import lax
from jax.sharding import PartitionSpec as P

BLK_DEV = 1


def accumulate(partial_value, pieces, targets, begin, finish, base, amp_rows):

    def step(slot, acc):
        piece = lax.dynamic_index_in_dim(pieces, slot - base, 0, keepdims=False)
        term = lax.dot_general(
            amp_rows, piece, (((1,), (1,)), ((), ())), preferred_element_type=jnp.float32
        )
        where = targets[slot]
        current = lax.dynamic_index_in_dim(acc, where, 0, keepdims=False)
        return lax.dynamic_update_index_in_dim(acc, current + term, where, 0)

    return lax.fori_loop(begin, finish, step, partial_value)


def local(amplitudes, integrals, cd_tile, target, counts):
    col_count = lax.axis_size("col")
    row_id = lax.axis_index("row")
    col_id = lax.axis_index("col")
    tile_pair = cd_tile[col_id]
    mine = lax.dynamic_index_in_dim(amplitudes, tile_pair, 0, keepdims=False)
    slots = integrals.shape[0]
    row_block = integrals.shape[1]
    blocks = BLK_DEV * col_count
    device = row_id * col_count + col_id
    own_targets = lax.dynamic_slice_in_dim(target, device * slots, slots, 0)
    own_count = counts[device]
    gathered = lax.all_gather(mine, "row", axis=0, tiled=True)
    empty = jnp.zeros((blocks, gathered.shape[0], row_block), jnp.float32)
    result = accumulate(empty, integrals, own_targets, 0, own_count, 0, gathered)
    return lax.psum_scatter(result, "col", scatter_dimension=0, tiled=True)


def solution(mesh):
    in_specs = (P(None, "row", None), P(("row", "col"), None, None), P(), P(), P())
    out_specs = P(("row", "col"), None, None)
    return jax.shard_map(local, mesh=mesh, in_specs=in_specs, out_specs=out_specs, check_vma=False)
```

profile of v0, /device:TPU:1, one launch (start us, length us, event | category | flops | bytes accessed | tf_op | source)
XLA Modules:
  0.0 218.3 jit_solution(16240546911521973178)
XLA Ops:
  6.5 0.0 copy-start
  6.5 0.0 all-gather.3.cloned.1.call-start
  6.5 1.4 dynamic_slice.26
  9.8 0.0 copy-done
  9.8 0.7 constant_dynamic-slice_fusion.1
  10.5 0.0 all-gather.3.cloned.1.call-update
  10.5 0.0 reduce-scatter.4.cloned.1.call-start
  10.6 0.8 dynamic_slice.25
  11.4 1.3 dynamic_slice.24
  12.6 131.4 %all-gather.3.cloned.1.call-done = bf16[1,576,2500]{2,0,1:T(2,128)(2,1)} async-done(((bf16[1,3,2500]{2,0,1:T(2,128)(2,1)}), bf16[1,576,2500]{2,0,1:T(2,128)(2,1)}) %all-gather.3.cloned.1.call-update) | async-done | bytes 2880016 | tf_op jit(solution)/shard_map/all_gather | solution.py:35
  144.1 5.0 %copy.9 = bf16[1,576,2500]{2,1,0:T(8,128)(2,1)} copy(bf16[1,576,2500]{2,0,1:T(2,128)(2,1)} %all-gather.3.cloned.1.call-done) | data formatting | bytes 5760000
  149.1 0.1 broadcast_in_dim.7
  149.2 7.3 %while.10 = (s32[]{:T(128)}, f32[4,576,200]{1,2,0:T(8,128)S(1)}, s32[]{:T(128)}, s32[4]{0:T(128)S(1)}, bf16[4,200,2500]{2,1,0:T(8,128)(2,1)}, /*index=5*/bf16[57...) while((s32[]{:T(128)}, f32[4,576,200]{1,2,0:T(8,128)S(1)}, s32[]{:T(128)}, s32[4]{0:T(128)S(1)}, ...), condition=%wide.region_1.2_spmd, body=%wide.region_0.1_spmd.sunk | while | flops 576115200 | bytes 5918905 | solution.py:20
  149.9 0.6 dynamic_slice.39
  152.5 3.4 %fusion.12 = f32[4,576,200]{1,2,0:T(8,128)S(1)} fusion(f32[4,576,200]{1,2,0:T(8,128)S(1)} %get-tuple-element.99, s32[]{:T(128)S(6)} %select_n.31, bf16[576,2500]{1,0:T(8,128)(2,1)} %get-tuple-element.112, bf16[4,200,2500]{2,1,0:T(8,128)(2,1)} %get-tuple-element.111, s32[]{:T(128)S(6)} %select_n.30, f32[1,576,200]{1,2,0:T(8,128)S(1)} %constant_dynamic-slice_fusion.3), kind=kOutput, calls=%fused_computation.3.clone.1 | convolution fusion | flops 576115200 | bytes 4997128 | tf_op jit(solution)/shard_map/while/body/dot_general | solution.py:13
  156.5 0.0 copy-start.1
  156.6 1.3 copy-done.1
  157.9 0.0 reduce-scatter.4.cloned.1.call-update
  157.9 53.6 %reduce-scatter.4.cloned.1.call-done = f32[1,576,200]{1,2,0:T(8,128)} async-done(((f32[4,576,200]{1,2,0:T(8,128)}), f32[1,576,200]{1,2,0:T(8,128)}) %reduce-scatter.4.cloned.1.call-update) | async-done | bytes 460816
  (1 shorter events, 0.0 us)
Async XLA Ops:
  6.5 3.3 %copy-start = (bf16[96,3,2500]{2,0,1:T(8,128)(2,1)S(1)}, bf16[96,3,2500]{2,0,1:T(8,128)(2,1)}, u32[]{:S(2)}) copy-start(bf16[96,3,2500]{2,0,1:T(8,128)(2,1)} %param.7) | copy-start | bytes 4320004
  6.5 137.6 %all-gather.3.cloned.1.call-start = ((), (), s32[]{:S(2)}) async-start(), calls=%async_computation.1 | async-start | bytes 5928960 | tf_op jit(solution)/shard_map/all_gather | solution.py:35
  10.5 200.9 %reduce-scatter.4.cloned.1.call-start = ((), (), s32[]{:S(2)}) async-start(), calls=%async_computation.2 | async-start | bytes 2560000
  156.5 1.3 copy-start.1
Sparse Core Ops, SparseCore 0:
  11.1 132.9 all-gather.2
  158.0 53.4 reduce-scatter.3
where the time goes:
time: 219 us; the launch traced here: 218 us
  waiting for transfers between devices  185 us (84%)
  between operations  15.4 us (7%)
  local copies, waits for them, and re-layouts  11.1 us (5%)
  matrix products  3.44 us (2%)
  loops' own time  3.25 us (1%)
    all_gather x1, waiting for transfers between devices, local(): gathered = lax.all_gather(mine, 'row', axis=0, tiled=True)  131 us
    unnamed x3, waiting for transfers between devices  53.6 us
    unnamed x5, local copies, waits for them, and re-layouts  6.31 us
  transfers between devices with their start and end apart: 2, of which 2 were waited for; matrix products, arithmetic and copies ran while one was open for 1% of the time, Pallas kernels for 0%

commit v1 on v0

v1 whole, which is shorter than its diff:
```python
import jax
import jax.numpy as jnp
from jax import lax
from jax.experimental import pallas as pl
from jax.experimental.pallas import tpu as pltpu
from jax.sharding import PartitionSpec as P

MESH = pl.DeviceIdType.MESH
NY, NZ, NX = 8, 12, 4
ROWS = 3
KT = 20
TP = 2500
CDW = 96
PAIRS = 576
RB = 200
SLOTS = 4
SLAB = 128
SLABS = 5
TOP = 104
NT = (((1,), (1,)), ((), ()))


def block_order():
    order = []
    row = 0
    for half, index in (
        [(1, 0), (1, 1), (1, 2), (0, 0), (1, 3), (1, 4), (0, 1), (0, 2), (1, 5), (1, 6), (1, 7), (1, 8)]
        + [(0, 3), (0, 4), (1, 9), (1, 10), (1, 11), (0, 5), (0, 6), (0, 7)]
    ):
        order.append((half, index, row))
        row += 36 if half == 0 else 24
    return order


def distance(index):
    return -((index + 1) // 2) if index % 2 else index // 2


def kernel(
    cd_ref, target_ref, counts_ref, amp_hbm, int_hbm, out_ref,
    amp_v, int_v, shard_v, g0, g1, wide, a_f, a_b, perm, pidx,
    p_own, p_send, r_half_l, r_half_r, r_full_l, r_full_r,
    load_sem, p1_send, p1_recv, p2_send, p2_recv, sib_send, sib_recv, x_send, x_recv,
):
    row, col = lax.axis_index("row"), lax.axis_index("col")
    y, z, core = row // (2 * NZ), (row // 2) % NZ, row % 2

    def at(yy, zz, cc):
        return ((yy * NZ + zz) * 2 + cc, col)

    up, down = (y + 1) % NY, (y + NY - 1) % NY
    fwd, back = (z + 1) % NZ, (z + NZ - 1) % NZ
    right, left = (col + 1) % NX, (col + NX - 1) % NX
    sibling = at(y, z, 1 - core)
    y_up, y_down = at(up, z, core), at(down, z, core)
    z_up, z_down = at(y, fwd, core), at(y, back, core)
    x_right, x_left = (row, right), (row, left)

    load_amp = pltpu.make_async_copy(amp_hbm, amp_v, load_sem.at[0])
    load_int = pltpu.make_async_copy(int_hbm, int_v, load_sem.at[1])
    load_amp.start()
    load_int.start()

    barrier = pltpu.get_barrier_semaphore()
    for other in (sibling, y_up, y_down, z_up, z_down, x_right, x_left):
        pl.semaphore_signal(barrier, inc=1, device_id=other, device_id_type=MESH)

    shard_v[...] = jnp.zeros_like(shard_v)
    apart = jnp.abs(lax.broadcasted_iota(jnp.int32, (16, CDW), 1) - cd_ref[col])
    one_hot = (1 - jnp.minimum(apart, 1)).astype(jnp.float32).astype(jnp.bfloat16)
    load_amp.wait()
    for p in range(ROWS):
        line = jnp.dot(one_hot, amp_v[p], preferred_element_type=jnp.float32)
        for k in range(KT):
            width = min(128, TP - 128 * k)
            shard_v[p * KT + k : p * KT + k + 1, 0:width] = line[0:1, 128 * k : 128 * k + width]
    packed = shard_v[...].astype(jnp.bfloat16)

    @pl.when(core == 0)
    def _():
        g0[y, z] = packed

    @pl.when(core == 1)
    def _():
        g1[z, y] = packed

    pl.semaphore_wait(barrier, 7)

    def copy(src, dst, send, recv, device):
        return pltpu.make_async_remote_copy(
            src_ref=src, dst_ref=dst, send_sem=send, recv_sem=recv, device_id=device, device_id_type=MESH
        )

    def ring1(buf, place, n, me, ahead, behind):
        def step(s, sign):
            i = (me - sign * (s - 1) + n) % n
            ref = buf.at[place(i)]
            d = 0 if sign > 0 else 1
            return copy(ref, ref, p1_send.at[d, s - 1], p1_recv.at[d, s - 1], ahead if sign > 0 else behind)

        for s in range(1, n // 2 + 1):
            step(s, 1).start()
            if s < n // 2:
                step(s, -1).start()
            step(s, 1).wait_recv()
            if s < n // 2:
                step(s, -1).wait_recv()
        for s in range(1, n // 2 + 1):
            step(s, 1).wait_send()
            if s < n // 2:
                step(s, -1).wait_send()

    def ring2(buf, n, me, inner, ahead, behind):
        def step(s, sign):
            i = (me - sign * (s - 1) + n) % n
            d = 0 if sign > 0 else 1
            ref = buf.at[i]
            if s == n // 2:
                ref = ref.at[pl.ds(0 if sign > 0 else inner // 2, inner // 2)]
            return copy(ref, ref, p2_send.at[d, s - 1], p2_recv.at[d, s - 1], ahead if sign > 0 else behind)

        return step

    y_step = ring2(g0, NY, y, NZ, y_up, y_down)
    z_step = ring2(g1, NZ, z, NY, z_up, z_down)

    def block_at(half, index):
        n, me = (NY, y) if half == 0 else (NZ, z)
        return (me + distance(index) + n) % n

    def to_sibling(half, index):
        ref = (g0 if half == 0 else g1).at[block_at(half, index)]
        return copy(ref, ref, sib_send.at[index], sib_recv.at[index], sibling)

    @pl.when(core == 0)
    def _():
        ring1(g0, lambda i: (y, i), NZ, z, z_up, z_down)
        y_step(1, 1).start()
        y_step(1, -1).start()
        to_sibling(0, 0).start()

    @pl.when(core == 1)
    def _():
        ring1(g1, lambda i: (z, i), NY, y, y_up, y_down)
        z_step(1, 1).start()
        z_step(1, -1).start()
        to_sibling(1, 0).start()

    def arrive(half, s):
        n, step = (NY, y_step) if half == 0 else (NZ, z_step)

        @pl.when(core == half)
        def _():
            for sign in (1, -1):
                step(s, sign).wait_recv()
                if s < n // 2:
                    step(s + 1, sign).start()
                    to_sibling(half, 2 * s - (1 if sign > 0 else 0)).start()
            if s == n // 2:
                to_sibling(half, 2 * s - 1).start()

    device = row * NX + col
    count = counts_ref[device]
    weights = []
    for d in range(NX):
        owner = (col + d) % NX
        line = []
        for q in range(SLOTS):
            live = jnp.minimum(jnp.maximum(count - q, 0), 1)
            same = 1 - jnp.minimum(jnp.abs(target_ref[device * SLOTS + q] - owner), 1)
            line.append((live * same).astype(jnp.float32))
        weights.append(line)

    order = block_order()
    pidx[...] = jnp.full_like(pidx, -1)
    for half, index, first in order:
        if half == 0:
            for r in range(ROWS):
                step = lax.broadcasted_iota(jnp.int32, (NZ, 128), 0)
                pidx[first + NZ * r : first + NZ * r + NZ, :] = block_at(0, index) * 72 + r + 6 * step
        else:
            for r in range(ROWS):
                step = lax.broadcasted_iota(jnp.int32, (NY, 128), 0)
                pidx[first + NY * r : first + NY * r + NY, :] = block_at(1, index) * 6 + 3 + r + 72 * step
    for t in range(SLABS):
        lanes = lax.broadcasted_iota(jnp.int32, (SLAB * SLABS, 128), 1) + 128 * t
        perm[:, 128 * t : 128 * t + 128] = jnp.where(pidx[...] == lanes, 1.0, 0.0).astype(jnp.bfloat16)
    a_f[:, PAIRS:, :] = jnp.zeros((KT, SLAB * SLABS - PAIRS, 128), jnp.float32)

    def unpack(half, index, first):
        n = NZ if half == 0 else NY
        i = block_at(half, index)

        @pl.when(core != half)
        def _():
            to_sibling(half, index).wait_recv()

        block = (g0 if half == 0 else g1)[i]
        wide[0 : n * 64, :] = block.reshape(n * 64, 128).astype(jnp.float32)

        @pl.loop(0, KT)
        def _(k):
            for r in range(ROWS):
                a_f[k, first + n * r : first + n * r + n, :] = wide[pl.ds(r * KT + k, n, stride=64), :]

    def x_copy(j, i):
        lo, hi = pl.ds(0, TOP), pl.ds(TOP, RB - TOP)
        src, dst = [
            (p_send.at[1, j, lo], r_half_l.at[j]),
            (p_send.at[1, j, hi], r_half_r.at[j]),
            (p_send.at[0, j, hi], r_full_l.at[j, hi]),
            (p_send.at[2, j, lo], r_full_r.at[j, lo]),
            (p_send.at[0, j, lo], r_full_l.at[j, lo]),
            (p_send.at[2, j, hi], r_full_r.at[j, hi]),
        ][i]
        return copy(src, dst, x_send.at[j, i], x_recv.at[j, i], x_left if i % 2 else x_right)

    def slab(j):
        for k in range(KT):
            a_b[:, 128 * k : 128 * k + 128] = a_f[k, SLAB * j : SLAB * j + SLAB, :].astype(jnp.bfloat16)
        terms = [
            lax.dot_general(int_v[q], a_b[:, 0:TP], NT, preferred_element_type=jnp.float32) for q in range(SLOTS)
        ]

        def part(d):
            return sum(w * t for w, t in zip(weights[d], terms))

        p_send[1, j] = part(2)
        x_copy(j, 0).start()
        x_copy(j, 1).start()
        p_send[0, j] = part(1)
        x_copy(j, 2).start()
        p_send[2, j] = part(3)
        x_copy(j, 3).start()
        p_own[j] = part(0)

    def relay(j):
        x_copy(j, 0).wait_recv()
        p_send[0, j, 0:TOP] = p_send[0, j, 0:TOP] + r_half_l[j]
        x_copy(j, 4).start()
        x_copy(j, 1).wait_recv()
        p_send[2, j, TOP:RB] = p_send[2, j, TOP:RB] + r_half_r[j]
        x_copy(j, 5).start()

    def finish(j):
        for i in range(2, 6):
            x_copy(j, i).wait_recv()
        whole = p_own[j] + r_full_l[j] + r_full_r[j]
        high = whole.astype(jnp.bfloat16)
        low = (whole - high.astype(jnp.float32)).astype(jnp.bfloat16)
        mine = perm[SLAB * j : SLAB * j + SLAB, 0:PAIRS]
        more = jnp.dot(high, mine, preferred_element_type=jnp.float32)
        more = more + jnp.dot(low, mine, preferred_element_type=jnp.float32)
        if j == 0:
            out_ref[...] = more
        else:
            out_ref[...] = out_ref[...] + more

    at_row = {(h, i): f for h, i, f in order}

    def take(*blocks):
        for b in blocks:
            unpack(*b, at_row[b])

    take((1, 0))
    arrive(1, 1)
    take((1, 1), (1, 2))
    take((0, 0))
    arrive(0, 1)
    arrive(1, 2)
    take((1, 3), (1, 4))
    load_int.wait()
    slab(0)
    arrive(0, 2)
    arrive(1, 3)
    take((0, 1), (0, 2))
    take((1, 5), (1, 6))
    slab(1)
    relay(0)
    arrive(1, 4)
    take((1, 7), (1, 8))
    arrive(0, 3)
    take((0, 3), (0, 4))
    arrive(1, 5)
    slab(2)
    relay(1)
    arrive(1, 6)
    arrive(0, 4)
    take((1, 9), (1, 10), (1, 11))
    take((0, 5), (0, 6))
    slab(3)
    relay(2)
    take((0, 7))
    slab(4)
    relay(3)
    finish(0)
    finish(1)
    relay(4)
    finish(2)
    finish(3)
    finish(4)

    @pl.when(core == 0)
    def _():
        for s in range(1, NY // 2 + 1):
            y_step(s, 1).wait_send()
            y_step(s, -1).wait_send()
        for index in range(NY):
            to_sibling(0, index).wait_send()

    @pl.when(core == 1)
    def _():
        for s in range(1, NZ // 2 + 1):
            z_step(s, 1).wait_send()
            z_step(s, -1).wait_send()
        for index in range(NZ):
            to_sibling(1, index).wait_send()

    for j in range(SLABS):
        for i in range(6):
            x_copy(j, i).wait_send()


def local(amplitudes, integrals, cd_tile, target, counts):
    amp = jnp.transpose(amplitudes, (1, 0, 2))
    anywhere, scalars = pl.BlockSpec(memory_space=pl.ANY), pl.BlockSpec(memory_space=pltpu.SMEM)
    dma = pltpu.SemaphoreType.DMA
    residual = pl.pallas_call(
        kernel,
        out_shape=jax.ShapeDtypeStruct((RB, PAIRS), jnp.float32),
        in_specs=[scalars, scalars, scalars, anywhere, anywhere],
        out_specs=pl.BlockSpec(memory_space=pltpu.VMEM),
        scratch_shapes=[
            pltpu.VMEM(amp.shape, jnp.bfloat16),
            pltpu.VMEM(integrals.shape, jnp.bfloat16),
            pltpu.VMEM((64, 128), jnp.float32),
            pltpu.VMEM((NY, NZ, 64, 128), jnp.bfloat16),
            pltpu.VMEM((NZ, NY, 64, 128), jnp.bfloat16),
            pltpu.VMEM((NZ * 64, 128), jnp.float32),
            pltpu.VMEM((KT, SLAB * SLABS, 128), jnp.float32),
            pltpu.VMEM((SLAB, KT * 128), jnp.bfloat16),
            pltpu.VMEM((SLAB * SLABS, SLAB * SLABS), jnp.bfloat16),
            pltpu.VMEM((SLAB * SLABS, 128), jnp.int32),
            pltpu.VMEM((SLABS, RB, SLAB), jnp.float32),
            pltpu.VMEM((3, SLABS, RB, SLAB), jnp.float32),
            pltpu.VMEM((SLABS, TOP, SLAB), jnp.float32),
            pltpu.VMEM((SLABS, RB - TOP, SLAB), jnp.float32),
            pltpu.VMEM((SLABS, RB, SLAB), jnp.float32),
            pltpu.VMEM((SLABS, RB, SLAB), jnp.float32),
            dma((2,)),
            dma((2, 6)),
            dma((2, 6)),
            dma((2, 6)),
            dma((2, 6)),
            dma((12,)),
            dma((12,)),
            dma((SLABS, 6)),
            dma((SLABS, 6)),
        ],
        compiler_params=pltpu.CompilerParams(
            collective_id=0, has_side_effects=True, vmem_limit_bytes=56 * 1024 * 1024
        ),
        cost_estimate=pl.CostEstimate(flops=2 * SLOTS * RB * PAIRS * TP, bytes_accessed=6 * 10**6, transcendentals=0),
    )(cd_tile, target, counts, amp, integrals)
    return jnp.transpose(residual)[None]


def solution(mesh):
    in_specs = (P(None, "row", None), P(("row", "col"), None, None), P(), P(), P())
    out_specs = P(("row", "col"), None, None)
    return jax.shard_map(local, mesh=mesh, in_specs=in_specs, out_specs=out_specs, check_vma=False)
```

time: 219 us -> 74 us (0.34)
  the two profiles are of different devices: /device:TPU:1 before, /device:TPU:2 now
where the time goes in v1:
time: 74 us; the launch traced here: 73.8 us
  Pallas kernels  71.9 us (97%)
  local copies, waits for them, and re-layouts  1.86 us (3%)
    pallas_call x1, Pallas kernels, local(): pl.pallas_call(kernel, out_shape=jax.ShapeDtypeStruct((RB, PAIRS), jnp.fl...  71.9 us
    unnamed x1, local copies, waits for them, and re-layouts  1.86 us

profile of v1, /device:TPU:2, one launch (start us, length us, event | category | flops | bytes accessed | tf_op | source)
XLA Modules:
  0.0 73.8 jit_solution(17490715869676418433)
XLA Ops:
  0.0 71.9 %shard_map.55 = f32[200,576]{1,0:T(8,128)} custom-call(s32[4]{0:T(128)} %cd_ref.1, s32[3072]{0:T(1024)} %target_ref.1, s32[768]{0:T(1024)} %counts_ref.1, bf16[3,96,2500]{2,1,0:T(8,128)(2,1)} %bitcast.5, bf16[4,200,2500]{2,1,0:T(8,128)(2,1)} %int_hbm.1), custom_call_target="tpu_custom_call" | custom-call | flops 2304000000 | bytes 6000000 | tf_op jit(solution)/shard_map/pallas_call | solution.py:328
  71.9 1.9 %copy.7 = f32[1,576,200]{1,2,0:T(8,128)} copy(f32[1,576,200]{1,2,0:T(8,128)} %bitcast.4) | data formatting | bytes 921600

commit v2 on v1

--- a/solution.py
+++ b/solution.py
@@ -14,9 +14,11 @@
 PAIRS = 576
 RB = 200
 SLOTS = 4
+Y_REACH, Z_REACH = 2, 3
 SLAB = 128
 SLABS = 5
-TOP = 104
+CODED = 208
+LEVELS = 32000.0
 NT = (((1,), (1,)), ((), ()))
 
 
@@ -24,8 +26,8 @@
     order = []
     row = 0
     for half, index in (
-        [(1, 0), (1, 1), (1, 2), (0, 0), (1, 3), (1, 4), (0, 1), (0, 2), (1, 5), (1, 6), (1, 7), (1, 8)]
-        + [(0, 3), (0, 4), (1, 9), (1, 10), (1, 11), (0, 5), (0, 6), (0, 7)]
+        [(1, 0), (0, 0), (1, 1), (1, 2), (1, 3), (1, 4), (0, 1), (0, 2), (1, 5), (1, 6), (0, 3), (0, 4)]
+        + [(1, 7), (1, 8), (0, 5), (0, 6), (1, 9), (1, 10), (1, 11), (0, 7)]
     ):
         order.append((half, index, row))
         row += 36 if half == 0 else 24
@@ -39,7 +41,7 @@
 def kernel(
     cd_ref, target_ref, counts_ref, amp_hbm, int_hbm, out_ref,
     amp_v, int_v, shard_v, g0, g1, wide, a_f, a_b, perm, pidx,
-    p_own, p_send, r_half_l, r_half_r, r_full_l, r_full_r,
+    p_own, p_send, p_got,
     load_sem, p1_send, p1_recv, p2_send, p2_recv, sib_send, sib_recv, x_send, x_recv,
 ):
     row, col = lax.axis_index("row"), lax.axis_index("col")
@@ -48,13 +50,16 @@
     def at(yy, zz, cc):
         return ((yy * NZ + zz) * 2 + cc, col)
 
-    up, down = (y + 1) % NY, (y + NY - 1) % NY
-    fwd, back = (z + 1) % NZ, (z + NZ - 1) % NZ
-    right, left = (col + 1) % NX, (col + NX - 1) % NX
+    def along_y(k):
+        return at((y + k + NY) % NY, z, core)
+
+    def along_z(k):
+        return at(y, (z + k + NZ) % NZ, core)
+
     sibling = at(y, z, 1 - core)
-    y_up, y_down = at(up, z, core), at(down, z, core)
-    z_up, z_down = at(y, fwd, core), at(y, back, core)
-    x_right, x_left = (row, right), (row, left)
+    def along_x(k):
+        return (row, (col + k) % NX)
+
 
     load_amp = pltpu.make_async_copy(amp_hbm, amp_v, load_sem.at[0])
     load_int = pltpu.make_async_copy(int_hbm, int_v, load_sem.at[1])
@@ -62,8 +67,23 @@
     load_int.start()
 
     barrier = pltpu.get_barrier_semaphore()
-    for other in (sibling, y_up, y_down, z_up, z_down, x_right, x_left):
-        pl.semaphore_signal(barrier, inc=1, device_id=other, device_id_type=MESH)
+
+    def greet(others):
+        for other in others:
+            pl.semaphore_signal(barrier, inc=1, device_id=other, device_id_type=MESH)
+
+    def reach(n, r):
+        return [k for s in range(r, 0, -1) for k in (s, -s)]
+
+    greet([sibling] + [along_x(k) for k in range(1, NX)])
+
+    @pl.when(core == 0)
+    def _():
+        greet([along_z(k) for k in range(1, NZ)] + [along_y(k) for k in reach(NY, Y_REACH)])
+
+    @pl.when(core == 1)
+    def _():
+        greet([along_y(k) for k in range(1, NY)] + [along_z(k) for k in reach(NZ, Z_REACH)])
 
     shard_v[...] = jnp.zeros_like(shard_v)
     apart = jnp.abs(lax.broadcasted_iota(jnp.int32, (16, CDW), 1) - cd_ref[col])
@@ -79,50 +99,37 @@
     @pl.when(core == 0)
     def _():
         g0[y, z] = packed
+        pl.semaphore_wait(barrier, NX + NZ - 1 + 2 * Y_REACH)
 
     @pl.when(core == 1)
     def _():
         g1[z, y] = packed
-
-    pl.semaphore_wait(barrier, 7)
+        pl.semaphore_wait(barrier, NX + NY - 1 + 2 * Z_REACH)
 
     def copy(src, dst, send, recv, device):
         return pltpu.make_async_remote_copy(
             src_ref=src, dst_ref=dst, send_sem=send, recv_sem=recv, device_id=device, device_id_type=MESH
         )
 
-    def ring1(buf, place, n, me, ahead, behind):
+    def ring1(ref, n, to):
+        copies = [copy(ref, ref, p1_send.at[k - 1], p1_recv.at[k - 1], to(k)) for k in range(1, n)]
+        for k in sorted(range(1, n), key=lambda k: abs(k - n // 2)):
+            copies[k - 1].start()
+        return copies
+
+    def ring2(buf, n, me, inner, far, to):
         def step(s, sign):
-            i = (me - sign * (s - 1) + n) % n
-            ref = buf.at[place(i)]
-            d = 0 if sign > 0 else 1
-            return copy(ref, ref, p1_send.at[d, s - 1], p1_recv.at[d, s - 1], ahead if sign > 0 else behind)
-
-        for s in range(1, n // 2 + 1):
-            step(s, 1).start()
-            if s < n // 2:
-                step(s, -1).start()
-            step(s, 1).wait_recv()
-            if s < n // 2:
-                step(s, -1).wait_recv()
-        for s in range(1, n // 2 + 1):
-            step(s, 1).wait_send()
-            if s < n // 2:
-                step(s, -1).wait_send()
-
-    def ring2(buf, n, me, inner, ahead, behind):
-        def step(s, sign):
-            i = (me - sign * (s - 1) + n) % n
+            i, hop = (me, s) if s <= far else ((me - sign * far + n) % n, s - far)
             d = 0 if sign > 0 else 1
             ref = buf.at[i]
             if s == n // 2:
                 ref = ref.at[pl.ds(0 if sign > 0 else inner // 2, inner // 2)]
-            return copy(ref, ref, p2_send.at[d, s - 1], p2_recv.at[d, s - 1], ahead if sign > 0 else behind)
+            return copy(ref, ref, p2_send.at[d, s - 1], p2_recv.at[d, s - 1], to(sign * hop))
 
         return step
 
-    y_step = ring2(g0, NY, y, NZ, y_up, y_down)
-    z_step = ring2(g1, NZ, z, NY, z_up, z_down)
+    y_step = ring2(g0, NY, y, NZ, Y_REACH, along_y)
+    z_step = ring2(g1, NZ, z, NY, Z_REACH, along_z)
 
     def block_at(half, index):
         n, me = (NY, y) if half == 0 else (NZ, z)
@@ -132,29 +139,39 @@
         ref = (g0 if half == 0 else g1).at[block_at(half, index)]
         return copy(ref, ref, sib_send.at[index], sib_recv.at[index], sibling)
 
+    def first(half):
+        if half == 0:
+            copies, step, far = ring1(g0.at[y, z], NZ, along_z), y_step, Y_REACH
+        else:
+            copies, step, far = ring1(g1.at[z, y], NY, along_y), z_step, Z_REACH
+        for c in copies:
+            c.wait_recv()
+        for s in range(far, 0, -1):
+            step(s, 1).start()
+            step(s, -1).start()
+        to_sibling(half, 0).start()
+        for c in copies:
+            c.wait_send()
+
     @pl.when(core == 0)
     def _():
-        ring1(g0, lambda i: (y, i), NZ, z, z_up, z_down)
-        y_step(1, 1).start()
-        y_step(1, -1).start()
-        to_sibling(0, 0).start()
+        first(0)
 
     @pl.when(core == 1)
     def _():
-        ring1(g1, lambda i: (z, i), NY, y, y_up, y_down)
-        z_step(1, 1).start()
-        z_step(1, -1).start()
-        to_sibling(1, 0).start()
+        first(1)
 
     def arrive(half, s):
-        n, step = (NY, y_step) if half == 0 else (NZ, z_step)
+        n, step, far = (NY, y_step, Y_REACH) if half == 0 else (NZ, z_step, Z_REACH)
 
         @pl.when(core == half)
         def _():
             for sign in (1, -1):
                 step(s, sign).wait_recv()
+                if s == far:
+                    for more in range(n // 2, far, -1):
+                        step(more, sign).start()
                 if s < n // 2:
-                    step(s + 1, sign).start()
                     to_sibling(half, 2 * s - (1 if sign > 0 else 0)).start()
             if s == n // 2:
                 to_sibling(half, 2 * s - 1).start()
@@ -203,17 +220,20 @@
             for r in range(ROWS):
                 a_f[k, first + n * r : first + n * r + n, :] = wide[pl.ds(r * KT + k, n, stride=64), :]
 
-    def x_copy(j, i):
-        lo, hi = pl.ds(0, TOP), pl.ds(TOP, RB - TOP)
-        src, dst = [
-            (p_send.at[1, j, lo], r_half_l.at[j]),
-            (p_send.at[1, j, hi], r_half_r.at[j]),
-            (p_send.at[0, j, hi], r_full_l.at[j, hi]),
-            (p_send.at[2, j, lo], r_full_r.at[j, lo]),
-            (p_send.at[0, j, lo], r_full_l.at[j, lo]),
-            (p_send.at[2, j, hi], r_full_r.at[j, hi]),
-        ][i]
-        return copy(src, dst, x_send.at[j, i], x_recv.at[j, i], x_left if i % 2 else x_right)
+    def x_copy(j, d):
+        return copy(p_send.at[d - 1, j], p_got.at[d - 1, j], x_send.at[j, d - 1], x_recv.at[j, d - 1], along_x(d))
+
+    def encode(part):
+        top = jnp.maximum(jnp.max(jnp.abs(part), axis=0, keepdims=True), 2.0**-110)
+        e = jnp.ceil(jnp.log2(top) * 64.0)
+        codes = jnp.round(part * (jnp.exp2(e * (-1 / 64)) * LEVELS)).astype(jnp.int32)
+        scale = jnp.broadcast_to(e.astype(jnp.int32), (CODED - RB, SLAB))
+        return jnp.concatenate([codes, scale], axis=0).astype(jnp.int16)
+
+    def decode(coded):
+        wide = coded.astype(jnp.int32)
+        scale = jnp.exp2(wide[RB : RB + 1].astype(jnp.float32) * (1 / 64)) * (1 / LEVELS)
+        return wide[0:RB].astype(jnp.float32) * scale
 
     def slab(j):
         for k in range(KT):
@@ -225,27 +245,16 @@
         def part(d):
             return sum(w * t for w, t in zip(weights[d], terms))
 
-        p_send[1, j] = part(2)
-        x_copy(j, 0).start()
-        x_copy(j, 1).start()
-        p_send[0, j] = part(1)
-        x_copy(j, 2).start()
-        p_send[2, j] = part(3)
-        x_copy(j, 3).start()
+        for d in (2, 1, 3):
+            p_send[d - 1, j] = encode(part(d))
+            x_copy(j, d).start()
         p_own[j] = part(0)
 
-    def relay(j):
-        x_copy(j, 0).wait_recv()
-        p_send[0, j, 0:TOP] = p_send[0, j, 0:TOP] + r_half_l[j]
-        x_copy(j, 4).start()
-        x_copy(j, 1).wait_recv()
-        p_send[2, j, TOP:RB] = p_send[2, j, TOP:RB] + r_half_r[j]
-        x_copy(j, 5).start()
-
     def finish(j):
-        for i in range(2, 6):
-            x_copy(j, i).wait_recv()
-        whole = p_own[j] + r_full_l[j] + r_full_r[j]
+        whole = p_own[j]
+        for d in (1, 3, 2):
+            x_copy(j, d).wait_recv()
+            whole = whole + decode(p_got[d - 1, j])
         high = whole.astype(jnp.bfloat16)
         low = (whole - high.astype(jnp.float32)).astype(jnp.bfloat16)
         mine = perm[SLAB * j : SLAB * j + SLAB, 0:PAIRS]
@@ -262,43 +271,33 @@
         for b in blocks:
             unpack(*b, at_row[b])
 
-    take((1, 0))
+    take((1, 0), (0, 0))
+    arrive(1, 3)
+    arrive(0, 2)
+    arrive(1, 2)
+    arrive(0, 1)
     arrive(1, 1)
-    take((1, 1), (1, 2))
-    take((0, 0))
-    arrive(0, 1)
-    arrive(1, 2)
-    take((1, 3), (1, 4))
+    take((1, 1), (1, 2), (1, 3), (1, 4))
     load_int.wait()
     slab(0)
-    arrive(0, 2)
-    arrive(1, 3)
     take((0, 1), (0, 2))
     take((1, 5), (1, 6))
     slab(1)
-    relay(0)
     arrive(1, 4)
-    take((1, 7), (1, 8))
     arrive(0, 3)
     take((0, 3), (0, 4))
+    take((1, 7), (1, 8))
+    slab(2)
     arrive(1, 5)
-    slab(2)
-    relay(1)
     arrive(1, 6)
     arrive(0, 4)
-    take((1, 9), (1, 10), (1, 11))
     take((0, 5), (0, 6))
+    take((1, 9), (1, 10))
     slab(3)
-    relay(2)
-    take((0, 7))
+    take((1, 11), (0, 7))
     slab(4)
-    relay(3)
-    finish(0)
-    finish(1)
-    relay(4)
-    finish(2)
-    finish(3)
-    finish(4)
+    for j in range(SLABS):
+        finish(j)
 
     @pl.when(core == 0)
     def _():
@@ -317,8 +316,8 @@
             to_sibling(1, index).wait_send()
 
     for j in range(SLABS):
-        for i in range(6):
-            x_copy(j, i).wait_send()
+        for d in range(1, NX):
+            x_copy(j, d).wait_send()
 
 
 def local(amplitudes, integrals, cd_tile, target, counts):
@@ -342,20 +341,17 @@
             pltpu.VMEM((SLAB * SLABS, SLAB * SLABS), jnp.bfloat16),
             pltpu.VMEM((SLAB * SLABS, 128), jnp.int32),
             pltpu.VMEM((SLABS, RB, SLAB), jnp.float32),
-            pltpu.VMEM((3, SLABS, RB, SLAB), jnp.float32),
-            pltpu.VMEM((SLABS, TOP, SLAB), jnp.float32),
-            pltpu.VMEM((SLABS, RB - TOP, SLAB), jnp.float32),
-            pltpu.VMEM((SLABS, RB, SLAB), jnp.float32),
-            pltpu.VMEM((SLABS, RB, SLAB), jnp.float32),
+            pltpu.VMEM((3, SLABS, CODED, SLAB), jnp.int16),
+            pltpu.VMEM((3, SLABS, CODED, SLAB), jnp.int16),
             dma((2,)),
-            dma((2, 6)),
-            dma((2, 6)),
+            dma((11,)),
+            dma((11,)),
             dma((2, 6)),
             dma((2, 6)),
             dma((12,)),
             dma((12,)),
-            dma((SLABS, 6)),
-            dma((SLABS, 6)),
+            dma((SLABS, 3)),
+            dma((SLABS, 3)),
         ],
         compiler_params=pltpu.CompilerParams(
             collective_id=0, has_side_effects=True, vmem_limit_bytes=56 * 1024 * 1024

time: 74 us -> 59.7 us (0.81)
  the two profiles are of different devices: /device:TPU:2 before, /device:TPU:1 now
where the time goes in v2:
time: 59.7 us; the launch traced here: 59.5 us
  Pallas kernels  57.6 us (96%)
  local copies, waits for them, and re-layouts  1.86 us (3%)
    pallas_call x1, Pallas kernels, local(): pl.pallas_call(kernel, out_shape=jax.ShapeDtypeStruct((RB, PAIRS), jnp.fl...  57.6 us
    unnamed x1, local copies, waits for them, and re-layouts  1.86 us

profile of v2, /device:TPU:1, one launch (start us, length us, event | category | flops | bytes accessed | tf_op | source)
XLA Modules:
  0.0 59.5 jit_solution(14851367821395755844)
XLA Ops:
  0.0 57.6 %shard_map.55 = f32[200,576]{1,0:T(8,128)} custom-call(s32[4]{0:T(128)} %cd_ref.1, s32[3072]{0:T(1024)} %target_ref.1, s32[768]{0:T(1024)} %counts_ref.1, bf16[3,96,2500]{2,1,0:T(8,128)(2,1)} %bitcast.5, bf16[4,200,2500]{2,1,0:T(8,128)(2,1)} %int_hbm.1), custom_call_target="tpu_custom_call" | custom-call | flops 2304000000 | bytes 6000000 | tf_op jit(solution)/shard_map/pallas_call | solution.py:327
  57.6 1.9 %copy.7 = f32[1,576,200]{1,2,0:T(8,128)} copy(f32[1,576,200]{1,2,0:T(8,128)} %bitcast.4) | data formatting | bytes 921600

commit v3 on v2

--- a/solution.py
+++ b/solution.py
@@ -15,9 +15,11 @@
 RB = 200
 SLOTS = 4
 Y_REACH, Z_REACH = 2, 3
+Z_NEAR, Y_NEAR = 7, 5
 SLAB = 128
 SLABS = 5
 CODED = 208
+FOLD, FOLDED = 104, 112
 LEVELS = 32000.0
 NT = (((1,), (1,)), ((), ()))
 
@@ -34,13 +36,17 @@
     return order
 
 
+def slot_of(k, n):
+    return 0 if k == 0 else 2 * k - 1 if k <= n // 2 else 2 * (n - k)
+
+
 def distance(index):
     return -((index + 1) // 2) if index % 2 else index // 2
 
 
 def kernel(
-    cd_ref, target_ref, counts_ref, amp_hbm, int_hbm, out_ref,
-    amp_v, int_v, shard_v, g0, g1, wide, a_f, a_b, perm, pidx,
+    cd_hbm, target_hbm, counts_hbm, amp_hbm, int_hbm, out_ref,
+    cd_ref, target_ref, counts_ref, amp_v, int_v, shard_v, g0, g1, wide, a_f, a_b, perm, pidx,
     p_own, p_send, p_got,
     load_sem, p1_send, p1_recv, p2_send, p2_recv, sib_send, sib_recv, x_send, x_recv,
 ):
@@ -63,8 +69,13 @@
 
     load_amp = pltpu.make_async_copy(amp_hbm, amp_v, load_sem.at[0])
     load_int = pltpu.make_async_copy(int_hbm, int_v, load_sem.at[1])
+    load_cd = pltpu.make_async_copy(cd_hbm, cd_ref, load_sem.at[2])
+    load_target = pltpu.make_async_copy(target_hbm, target_ref, load_sem.at[3])
+    load_counts = pltpu.make_async_copy(counts_hbm, counts_ref, load_sem.at[4])
+    load_cd.start()
     load_amp.start()
-    load_int.start()
+    load_target.start()
+    load_counts.start()
 
     barrier = pltpu.get_barrier_semaphore()
 
@@ -86,9 +97,11 @@
         greet([along_y(k) for k in range(1, NY)] + [along_z(k) for k in reach(NZ, Z_REACH)])
 
     shard_v[...] = jnp.zeros_like(shard_v)
+    load_cd.wait()
     apart = jnp.abs(lax.broadcasted_iota(jnp.int32, (16, CDW), 1) - cd_ref[col])
     one_hot = (1 - jnp.minimum(apart, 1)).astype(jnp.float32).astype(jnp.bfloat16)
     load_amp.wait()
+    load_int.start()
     for p in range(ROWS):
         line = jnp.dot(one_hot, amp_v[p], preferred_element_type=jnp.float32)
         for k in range(KT):
@@ -98,12 +111,12 @@
 
     @pl.when(core == 0)
     def _():
-        g0[y, z] = packed
+        g0[y, 0] = packed
         pl.semaphore_wait(barrier, NX + NZ - 1 + 2 * Y_REACH)
 
     @pl.when(core == 1)
     def _():
-        g1[z, y] = packed
+        g1[z, 0] = packed
         pl.semaphore_wait(barrier, NX + NY - 1 + 2 * Z_REACH)
 
     def copy(src, dst, send, recv, device):
@@ -111,25 +124,28 @@
             src_ref=src, dst_ref=dst, send_sem=send, recv_sem=recv, device_id=device, device_id_type=MESH
         )
 
-    def ring1(ref, n, to):
-        copies = [copy(ref, ref, p1_send.at[k - 1], p1_recv.at[k - 1], to(k)) for k in range(1, n)]
-        for k in sorted(range(1, n), key=lambda k: abs(k - n // 2)):
-            copies[k - 1].start()
+    def ring1(block, n, to):
+        own, copies = block.at[0], {}
+        for k in sorted(range(1, n), key=lambda k: min(k, n - k)):
+            place = block.at[slot_of(n - k, n)]
+            copies[k] = copy(own, place, p1_send.at[k - 1], p1_recv.at[k - 1], to(k))
+            copies[k].start()
         return copies
 
-    def ring2(buf, n, me, inner, far, to):
-        def step(s, sign):
+    def ring2(buf, n, me, inner, near, far, to):
+        def step(s, sign, piece):
             i, hop = (me, s) if s <= far else ((me - sign * far + n) % n, s - far)
             d = 0 if sign > 0 else 1
-            ref = buf.at[i]
-            if s == n // 2:
-                ref = ref.at[pl.ds(0 if sign > 0 else inner // 2, inner // 2)]
-            return copy(ref, ref, p2_send.at[d, s - 1], p2_recv.at[d, s - 1], to(sign * hop))
+            ref = buf.at[i, pl.ds(0, near) if piece == 0 else pl.ds(near, inner - near)]
+            return copy(ref, ref, p2_send.at[d, s - 1, piece], p2_recv.at[d, s - 1, piece], to(sign * hop))
 
         return step
 
-    y_step = ring2(g0, NY, y, NZ, Y_REACH, along_y)
-    z_step = ring2(g1, NZ, z, NY, Z_REACH, along_z)
+    def pieces(n, s, sign):
+        return (0, 1) if s < n // 2 else (0,) if sign > 0 else (1,)
+
+    y_step = ring2(g0, NY, y, NZ, Z_NEAR, Y_REACH, along_y)
+    z_step = ring2(g1, NZ, z, NY, Y_NEAR, Z_REACH, along_z)
 
     def block_at(half, index):
         n, me = (NY, y) if half == 0 else (NZ, z)
@@ -141,16 +157,19 @@
 
     def first(half):
         if half == 0:
-            copies, step, far = ring1(g0.at[y, z], NZ, along_z), y_step, Y_REACH
+            block, inner, to, step, n, far, near = g0.at[y], NZ, along_z, y_step, NY, Y_REACH, Z_NEAR
         else:
-            copies, step, far = ring1(g1.at[z, y], NY, along_y), z_step, Z_REACH
-        for c in copies:
-            c.wait_recv()
-        for s in range(far, 0, -1):
-            step(s, 1).start()
-            step(s, -1).start()
+            block, inner, to, step, n, far, near = g1.at[z], NY, along_y, z_step, NZ, Z_REACH, Y_NEAR
+        copies = ring1(block, inner, to)
+        for piece in (0, 1):
+            for k in range(1, inner):
+                if (slot_of(inner - k, inner) < near) == (piece == 0):
+                    copies[k].wait_recv()
+            for s in range(far, 0, -1):
+                for sign in (1, -1):
+                    step(s, sign, piece).start()
         to_sibling(half, 0).start()
-        for c in copies:
+        for c in copies.values():
             c.wait_send()
 
     @pl.when(core == 0)
@@ -161,21 +180,32 @@
     def _():
         first(1)
 
+    def second(half):
+        n, step, far = (NY, y_step, Y_REACH) if half == 0 else (NZ, z_step, Z_REACH)
+        for piece in (0, 1):
+            for sign in (1, -1):
+                step(far, sign, piece).wait_recv()
+                for more in range(n // 2, far, -1):
+                    if piece in pieces(n, more, sign):
+                        step(more, sign, piece).start()
+        for sign in (1, -1):
+            to_sibling(half, 2 * far - (1 if sign > 0 else 0)).start()
+
     def arrive(half, s):
-        n, step, far = (NY, y_step, Y_REACH) if half == 0 else (NZ, z_step, Z_REACH)
+        n, step = (NY, y_step) if half == 0 else (NZ, z_step)
 
         @pl.when(core == half)
         def _():
             for sign in (1, -1):
-                step(s, sign).wait_recv()
-                if s == far:
-                    for more in range(n // 2, far, -1):
-                        step(more, sign).start()
+                for piece in pieces(n, s, sign):
+                    step(s, sign, piece).wait_recv()
                 if s < n // 2:
                     to_sibling(half, 2 * s - (1 if sign > 0 else 0)).start()
             if s == n // 2:
                 to_sibling(half, 2 * s - 1).start()
 
+    load_target.wait()
+    load_counts.wait()
     device = row * NX + col
     count = counts_ref[device]
     weights = []
@@ -190,15 +220,18 @@
 
     order = block_order()
     pidx[...] = jnp.full_like(pidx, -1)
-    for half, index, first in order:
-        if half == 0:
-            for r in range(ROWS):
-                step = lax.broadcasted_iota(jnp.int32, (NZ, 128), 0)
-                pidx[first + NZ * r : first + NZ * r + NZ, :] = block_at(0, index) * 72 + r + 6 * step
-        else:
-            for r in range(ROWS):
-                step = lax.broadcasted_iota(jnp.int32, (NY, 128), 0)
-                pidx[first + NY * r : first + NY * r + NY, :] = block_at(1, index) * 6 + 3 + r + 72 * step
+    for half, index, first_row in order:
+        n, me = (NZ, z) if half == 0 else (NY, y)
+        place = lax.broadcasted_iota(jnp.int32, (n, 128), 0)
+        away = (place + 1) // 2
+        source = me + jnp.where(place % 2 == 1, away, -away)
+        source = jnp.where(source < 0, source + n, jnp.where(source >= n, source - n, source))
+        for r in range(ROWS):
+            if half == 0:
+                pair = block_at(0, index) * 72 + source * 6 + r
+            else:
+                pair = source * 72 + block_at(1, index) * 6 + 3 + r
+            pidx[first_row + n * r : first_row + n * r + n, :] = pair
     for t in range(SLABS):
         lanes = lax.broadcasted_iota(jnp.int32, (SLAB * SLABS, 128), 1) + 128 * t
         perm[:, 128 * t : 128 * t + 128] = jnp.where(pidx[...] == lanes, 1.0, 0.0).astype(jnp.bfloat16)
@@ -221,19 +254,30 @@
                 a_f[k, first + n * r : first + n * r + n, :] = wide[pl.ds(r * KT + k, n, stride=64), :]
 
     def x_copy(j, d):
-        return copy(p_send.at[d - 1, j], p_got.at[d - 1, j], x_send.at[j, d - 1], x_recv.at[j, d - 1], along_x(d))
-
-    def encode(part):
+        rows = pl.ds(0, CODED if j < SLABS - 1 else FOLDED)
+        src, dst = p_send.at[d - 1, j, rows], p_got.at[d - 1, j, rows]
+        return copy(src, dst, x_send.at[j, d - 1], x_recv.at[j, d - 1], along_x(d))
+
+    def encode(part, j):
         top = jnp.maximum(jnp.max(jnp.abs(part), axis=0, keepdims=True), 2.0**-110)
         e = jnp.ceil(jnp.log2(top) * 64.0)
         codes = jnp.round(part * (jnp.exp2(e * (-1 / 64)) * LEVELS)).astype(jnp.int32)
         scale = jnp.broadcast_to(e.astype(jnp.int32), (CODED - RB, SLAB))
+        if j == SLABS - 1:
+            lower = pltpu.roll(codes[FOLD:], 64, 1)
+            lower = jnp.concatenate([lower, jnp.zeros((2 * FOLD - RB, SLAB), jnp.int32)], axis=0)
+            codes = codes[0:FOLD] + lower
         return jnp.concatenate([codes, scale], axis=0).astype(jnp.int16)
 
-    def decode(coded):
-        wide = coded.astype(jnp.int32)
-        scale = jnp.exp2(wide[RB : RB + 1].astype(jnp.float32) * (1 / 64)) * (1 / LEVELS)
-        return wide[0:RB].astype(jnp.float32) * scale
+    def decode(d, j):
+        if j < SLABS - 1:
+            wide = p_got[d - 1, j].astype(jnp.int32)
+            codes, e = wide[0:RB], wide[RB : RB + 1]
+        else:
+            wide = p_got[d - 1, j, 0:FOLDED].astype(jnp.int32)
+            codes = jnp.concatenate([wide[0:FOLD], pltpu.roll(wide[0 : RB - FOLD], 64, 1)], axis=0)
+            e = wide[FOLD : FOLD + 1]
+        return codes.astype(jnp.float32) * (jnp.exp2(e.astype(jnp.float32) * (1 / 64)) * (1 / LEVELS))
 
     def slab(j):
         for k in range(KT):
@@ -246,7 +290,8 @@
             return sum(w * t for w, t in zip(weights[d], terms))
 
         for d in (2, 1, 3):
-            p_send[d - 1, j] = encode(part(d))
+            coded = encode(part(d), j)
+            p_send[d - 1, j, 0 : coded.shape[0]] = coded
             x_copy(j, d).start()
         p_own[j] = part(0)
 
@@ -254,7 +299,7 @@
         whole = p_own[j]
         for d in (1, 3, 2):
             x_copy(j, d).wait_recv()
-            whole = whole + decode(p_got[d - 1, j])
+            whole = whole + decode(d, j)
         high = whole.astype(jnp.bfloat16)
         low = (whole - high.astype(jnp.float32)).astype(jnp.bfloat16)
         mine = perm[SLAB * j : SLAB * j + SLAB, 0:PAIRS]
@@ -271,9 +316,15 @@
         for b in blocks:
             unpack(*b, at_row[b])
 
+    @pl.when(core == 0)
+    def _():
+        second(0)
+
+    @pl.when(core == 1)
+    def _():
+        second(1)
+
     take((1, 0), (0, 0))
-    arrive(1, 3)
-    arrive(0, 2)
     arrive(1, 2)
     arrive(0, 1)
     arrive(1, 1)
@@ -290,28 +341,31 @@
     slab(2)
     arrive(1, 5)
     arrive(1, 6)
+    finish(0)
     arrive(0, 4)
     take((0, 5), (0, 6))
     take((1, 9), (1, 10))
     slab(3)
     take((1, 11), (0, 7))
     slab(4)
-    for j in range(SLABS):
+    for j in range(1, SLABS):
         finish(j)
 
+    def sent(n, step):
+        for s in range(1, n // 2 + 1):
+            for sign in (1, -1):
+                for piece in pieces(n, s, sign):
+                    step(s, sign, piece).wait_send()
+
     @pl.when(core == 0)
     def _():
-        for s in range(1, NY // 2 + 1):
-            y_step(s, 1).wait_send()
-            y_step(s, -1).wait_send()
+        sent(NY, y_step)
         for index in range(NY):
             to_sibling(0, index).wait_send()
 
     @pl.when(core == 1)
     def _():
-        for s in range(1, NZ // 2 + 1):
-            z_step(s, 1).wait_send()
-            z_step(s, -1).wait_send()
+        sent(NZ, z_step)
         for index in range(NZ):
             to_sibling(1, index).wait_send()
 
@@ -322,14 +376,17 @@
 
 def local(amplitudes, integrals, cd_tile, target, counts):
     amp = jnp.transpose(amplitudes, (1, 0, 2))
-    anywhere, scalars = pl.BlockSpec(memory_space=pl.ANY), pl.BlockSpec(memory_space=pltpu.SMEM)
+    anywhere = pl.BlockSpec(memory_space=pl.ANY)
     dma = pltpu.SemaphoreType.DMA
     residual = pl.pallas_call(
         kernel,
         out_shape=jax.ShapeDtypeStruct((RB, PAIRS), jnp.float32),
-        in_specs=[scalars, scalars, scalars, anywhere, anywhere],
+        in_specs=[anywhere] * 5,
         out_specs=pl.BlockSpec(memory_space=pltpu.VMEM),
         scratch_shapes=[
+            pltpu.SMEM(cd_tile.shape, jnp.int32),
+            pltpu.SMEM(target.shape, jnp.int32),
+            pltpu.SMEM(counts.shape, jnp.int32),
             pltpu.VMEM(amp.shape, jnp.bfloat16),
             pltpu.VMEM(integrals.shape, jnp.bfloat16),
             pltpu.VMEM((64, 128), jnp.float32),
@@ -343,11 +400,11 @@
             pltpu.VMEM((SLABS, RB, SLAB), jnp.float32),
             pltpu.VMEM((3, SLABS, CODED, SLAB), jnp.int16),
             pltpu.VMEM((3, SLABS, CODED, SLAB), jnp.int16),
-            dma((2,)),
+            dma((5,)),
             dma((11,)),
             dma((11,)),
-            dma((2, 6)),
-            dma((2, 6)),
+            dma((2, 6, 2)),
+            dma((2, 6, 2)),
             dma((12,)),
             dma((12,)),
             dma((SLABS, 3)),

time: 59.7 us -> 57.7 us (0.966)
  the two profiles are of different devices: /device:TPU:1 before, /device:TPU:64 now
where the time goes in v3:
time: 57.7 us; the launch traced here: 57.5 us
  Pallas kernels  55.7 us (97%)
  local copies, waits for them, and re-layouts  1.86 us (3%)
    pallas_call x1, Pallas kernels, local(): pl.pallas_call(kernel, out_shape=jax.ShapeDtypeStruct((RB, PAIRS), jnp.fl...  55.7 us
    unnamed x1, local copies, waits for them, and re-layouts  1.86 us

profile of v3, /device:TPU:64, one launch (start us, length us, event | category | flops | bytes accessed | tf_op | source)
XLA Modules:
  0.0 57.5 jit_solution(15215011043093024952)
XLA Ops:
  0.0 55.7 %shard_map.55 = f32[200,576]{1,0:T(8,128)} custom-call(s32[4]{0:T(128)} %cd_hbm.1, s32[3072]{0:T(1024)} %target_hbm.1, s32[768]{0:T(1024)} %counts_hbm.1, bf16[3,96,2500]{2,1,0:T(8,128)(2,1)} %bitcast.5, bf16[4,200,2500]{2,1,0:T(8,128)(2,1)} %int_hbm.1), custom_call_target="tpu_custom_call" | custom-call | flops 2304000000 | bytes 6000000 | tf_op jit(solution)/shard_map/pallas_call | solution.py:381
  55.7 1.9 %copy.7 = f32[1,576,200]{1,2,0:T(8,128)} copy(f32[1,576,200]{1,2,0:T(8,128)} %bitcast.4) | data formatting | bytes 921600

commit v4 on v3

--- a/solution.py
+++ b/solution.py
@@ -15,7 +15,7 @@
 RB = 200
 SLOTS = 4
 Y_REACH, Z_REACH = 2, 3
-Z_NEAR, Y_NEAR = 7, 5
+Z_NEAR, Y_NEAR = 5, 3
 SLAB = 128
 SLABS = 5
 CODED = 208
@@ -248,7 +248,7 @@
         block = (g0 if half == 0 else g1)[i]
         wide[0 : n * 64, :] = block.reshape(n * 64, 128).astype(jnp.float32)
 
-        @pl.loop(0, KT)
+        @pl.loop(0, KT, unroll=5)
         def _(k):
             for r in range(ROWS):
                 a_f[k, first + n * r : first + n * r + n, :] = wide[pl.ds(r * KT + k, n, stride=64), :]
@@ -341,14 +341,13 @@
     slab(2)
     arrive(1, 5)
     arrive(1, 6)
-    finish(0)
     arrive(0, 4)
     take((0, 5), (0, 6))
     take((1, 9), (1, 10))
     slab(3)
     take((1, 11), (0, 7))
     slab(4)
-    for j in range(1, SLABS):
+    for j in range(SLABS):
         finish(j)
 
     def sent(n, step):

time: 57.7 us -> 56 us (0.971)
  the two profiles are of different devices: /device:TPU:64 before, /device:TPU:1 now
where the time goes in v4:
time: 56 us; the launch traced here: 55.8 us
  Pallas kernels  53.9 us (96%)
  local copies, waits for them, and re-layouts  1.86 us (3%)
    pallas_call x1, Pallas kernels, local(): pl.pallas_call(kernel, out_shape=jax.ShapeDtypeStruct((RB, PAIRS), jnp.fl...  53.9 us
    unnamed x1, local copies, waits for them, and re-layouts  1.86 us

profile of v4, /device:TPU:1, one launch (start us, length us, event | category | flops | bytes accessed | tf_op | source)
XLA Modules:
  0.0 55.8 jit_solution(16293331166139089992)
XLA Ops:
  0.0 53.9 %shard_map.55 = f32[200,576]{1,0:T(8,128)} custom-call(s32[4]{0:T(128)} %cd_hbm.1, s32[3072]{0:T(1024)} %target_hbm.1, s32[768]{0:T(1024)} %counts_hbm.1, bf16[3,96,2500]{2,1,0:T(8,128)(2,1)} %bitcast.5, bf16[4,200,2500]{2,1,0:T(8,128)(2,1)} %int_hbm.1), custom_call_target="tpu_custom_call" | custom-call | flops 2304000000 | bytes 6000000 | tf_op jit(solution)/shard_map/pallas_call | solution.py:380
  53.9 1.9 %copy.7 = f32[1,576,200]{1,2,0:T(8,128)} copy(f32[1,576,200]{1,2,0:T(8,128)} %bitcast.4) | data formatting | bytes 921600

commit v5 on v4

--- a/solution.py
+++ b/solution.py
@@ -331,8 +331,8 @@
     take((1, 1), (1, 2), (1, 3), (1, 4))
     load_int.wait()
     slab(0)
+    take((1, 5), (1, 6))
     take((0, 1), (0, 2))
-    take((1, 5), (1, 6))
     slab(1)
     arrive(1, 4)
     arrive(0, 3)

time: 56 us -> 56 us (level)
  no operation moved by 1% of the time
where the time goes in v5:
time: 56 us; the launch traced here: 55.8 us
  Pallas kernels  53.9 us (96%)
  local copies, waits for them, and re-layouts  1.86 us (3%)
    pallas_call x1, Pallas kernels, local(): pl.pallas_call(kernel, out_shape=jax.ShapeDtypeStruct((RB, PAIRS), jnp.fl...  53.9 us
    unnamed x1, local copies, waits for them, and re-layouts  1.86 us

profile of v5, /device:TPU:1, one launch (start us, length us, event | category | flops | bytes accessed | tf_op | source)
XLA Modules:
  0.0 55.8 jit_solution(3019759331399969943)
XLA Ops:
  0.0 53.9 %shard_map.55 = f32[200,576]{1,0:T(8,128)} custom-call(s32[4]{0:T(128)} %cd_hbm.1, s32[3072]{0:T(1024)} %target_hbm.1, s32[768]{0:T(1024)} %counts_hbm.1, bf16[3,96,2500]{2,1,0:T(8,128)(2,1)} %bitcast.5, bf16[4,200,2500]{2,1,0:T(8,128)(2,1)} %int_hbm.1), custom_call_target="tpu_custom_call" | custom-call | flops 2304000000 | bytes 6000000 | tf_op jit(solution)/shard_map/pallas_call | solution.py:380
  53.9 1.9 %copy.7 = f32[1,576,200]{1,2,0:T(8,128)} copy(f32[1,576,200]{1,2,0:T(8,128)} %bitcast.4) | data formatting | bytes 921600

commit v6 on v4

--- a/solution.py
+++ b/solution.py
@@ -248,7 +248,7 @@
         block = (g0 if half == 0 else g1)[i]
         wide[0 : n * 64, :] = block.reshape(n * 64, 128).astype(jnp.float32)
 
-        @pl.loop(0, KT, unroll=5)
+        @pl.loop(0, KT, unroll=10)
         def _(k):
             for r in range(ROWS):
                 a_f[k, first + n * r : first + n * r + n, :] = wide[pl.ds(r * KT + k, n, stride=64), :]

time: 56 us -> 55.9 us (level)
  no operation moved by 1% of the time
where the time goes in v6:
time: 55.9 us; the launch traced here: 55.7 us
  Pallas kernels  53.8 us (96%)
  local copies, waits for them, and re-layouts  1.86 us (3%)
    pallas_call x1, Pallas kernels, local(): pl.pallas_call(kernel, out_shape=jax.ShapeDtypeStruct((RB, PAIRS), jnp.fl...  53.8 us
    unnamed x1, local copies, waits for them, and re-layouts  1.86 us

profile of v6, /device:TPU:1, one launch (start us, length us, event | category | flops | bytes accessed | tf_op | source)
XLA Modules:
  0.0 55.7 jit_solution(16574266135198351803)
XLA Ops:
  0.0 53.8 %shard_map.55 = f32[200,576]{1,0:T(8,128)} custom-call(s32[4]{0:T(128)} %cd_hbm.1, s32[3072]{0:T(1024)} %target_hbm.1, s32[768]{0:T(1024)} %counts_hbm.1, bf16[3,96,2500]{2,1,0:T(8,128)(2,1)} %bitcast.5, bf16[4,200,2500]{2,1,0:T(8,128)(2,1)} %int_hbm.1), custom_call_target="tpu_custom_call" | custom-call | flops 2304000000 | bytes 6000000 | tf_op jit(solution)/shard_map/pallas_call | solution.py:380
  53.8 1.9 %copy.7 = f32[1,576,200]{1,2,0:T(8,128)} copy(f32[1,576,200]{1,2,0:T(8,128)} %bitcast.4) | data formatting | bytes 921600
